TPU v7x, 128 devices: a whole 4x4x4 slice. The times are simulated.
128 devices in a mesh: row: 8 (over x, core), col: 16 (over z, y).
Axes of the slice: x: 4, y: 4, z: 4, core: 2. Of those that a mesh axis runs over, the one named last changes fastest.
Arguments:
- density: bfloat16 [6144, 6144], P('row', 'col'), may hold values from -5 to 5
- strips: bfloat16 [16384, 8, 128], P(('row', 'col')), may hold values from -5 to 5
- dest_device: int32 [16384, 1], P(('row', 'col')), may hold values from 0 to 127; in each aligned block of 128 rows (0 to 127, 128 to 255, ...) at most 2 rows name the same one
- atom_slot: int32 [16384], P(('row', 'col')), may hold values from 0 to 95
- block_slot: int32 [16384], P(('row', 'col')), may hold values from 0 to 2
- patterns: int32 [3, 48, 48], replicated, may hold values 0 or 1
Outputs:
- density_next: float32 [6144, 6144], P('row', 'col')
- response_next: float32 [6144, 6144], P('row', 'col')
Inputs may be any that keep to these rules, and one draw needn't show every extreme that they name: `dest_device`: of the 128 strips of one device, at most 2 name the same owner, and some owner is named that often.
All inputs are finite; a program needn't handle non-finite values.
Results may differ from a plain program's by a relative error of at most 0.0036.
Values may be sent and summed in bfloat16 or wider, within the bound.
A program may use at most 128 MiB of HBM per device.

v0:
```python
import math
import jax
import jax.numpy as jnp
from jax import lax
from jax.sharding import PartitionSpec as P

STEPS = 2
CAPACITY = 2


def tile_kept(patterns, which, row_offset, col_offset, block_rows, block_cols, block_width):
    window = lax.dynamic_slice(patterns[which], (row_offset, col_offset), (block_rows, block_cols))
    global_rows = row_offset + lax.iota(jnp.int32, block_rows)
    global_cols = col_offset + lax.iota(jnp.int32, block_cols)
    diagonal = (global_rows[:, None] == global_cols[None, :]).astype(jnp.int32)
    kept = jnp.maximum(window, diagonal).astype(jnp.float32)
    return jnp.repeat(jnp.repeat(kept, block_width, axis=0), block_width, axis=1)


def products(zeroth, linear):
    col_zero, col_first = (
        lax.all_gather(zeroth, "row", axis=0, tiled=True),
        lax.all_gather(linear, "row", axis=0, tiled=True),
    )
    pieces = (
        lax.all_gather(zeroth, "col", axis=1, tiled=True),
        lax.all_gather(linear, "col", axis=1, tiled=True),
    )
    square = jnp.dot(pieces[0], col_zero, preferred_element_type=jnp.float32)
    left_part = jnp.dot(pieces[0], col_first, preferred_element_type=jnp.float32)
    right_part = jnp.dot(pieces[1], col_zero, preferred_element_type=jnp.float32)
    return (square, left_part + right_part)


def on_device(density, strips, dest_device, atom_slot, block_slot, patterns):
    tile_rows, tile_cols = density.shape
    mesh_rows = lax.axis_size("row")
    mesh_cols = lax.axis_size("col")
    devices = mesh_rows * mesh_cols
    matrix_order = tile_rows * mesh_rows
    atom_width = strips.shape[1]
    block_width = strips.shape[2]
    block_rows = tile_rows // block_width
    block_cols = tile_cols // block_width
    row_offset = lax.axis_index("row") * block_rows
    col_offset = lax.axis_index("col") * block_cols
    kept_zero = tile_kept(patterns, 0, row_offset, col_offset, block_rows, block_cols, block_width)
    kept_first = tile_kept(patterns, 1, row_offset, col_offset, block_rows, block_cols, block_width)
    kept_field = tile_kept(patterns, 2, row_offset, col_offset, block_rows, block_cols, block_width)
    capacity = CAPACITY
    targets = dest_device[:, 0]
    order = lax.iota(jnp.int32, targets.shape[0])
    earlier = (targets[:, None] == targets[None, :]) & (order[None, :] < order[:, None])
    ranking = jnp.sum(earlier.astype(jnp.int32), axis=1)
    position = targets * capacity + ranking
    sent_strips = (
        jnp.zeros((devices * capacity, atom_width, block_width), strips.dtype)
        .at[position]
        .set(strips)
    )
    sent_atoms = jnp.full((devices * capacity,), -1, jnp.int32).at[position].set(atom_slot)
    sent_blocks = jnp.zeros((devices * capacity,), jnp.int32).at[position].set(block_slot)
    arrived = (
        lax.all_to_all(
            sent_strips.reshape(devices, capacity, atom_width, block_width),
            ("row", "col"),
            split_axis=0,
            concat_axis=0,
            tiled=True,
        ),
        lax.all_to_all(
            sent_atoms.reshape(devices, capacity),
            ("row", "col"),
            split_axis=0,
            concat_axis=0,
            tiled=True,
        ),
        lax.all_to_all(
            sent_blocks.reshape(devices, capacity),
            ("row", "col"),
            split_axis=0,
            concat_axis=0,
            tiled=True,
        ),
    )
    recv_strips = arrived[0].reshape(-1, atom_width * block_width)
    recv_atoms = arrived[1].reshape(-1)
    recv_blocks = arrived[2].reshape(-1)
    atoms_here = tile_rows // atom_width
    atom_match = recv_atoms[:, None] == lax.iota(jnp.int32, atoms_here)[None, :]
    block_match = recv_blocks[:, None] == lax.iota(jnp.int32, block_cols)[None, :]
    placing = (
        (atom_match[:, :, None] & block_match[:, None, :])
        .astype(jnp.bfloat16)
        .reshape(-1, atoms_here * block_cols)
    )
    summed = lax.dot_general(
        placing, recv_strips, (((0,), (0,)), ((), ())), preferred_element_type=jnp.float32
    )
    h_field = (
        summed.reshape(atoms_here, block_cols, atom_width, block_width)
        .transpose(0, 2, 1, 3)
        .reshape(tile_rows, tile_cols)
    )
    linear = (-(kept_field * h_field)).astype(jnp.bfloat16)
    zeroth = density
    inv_root = 1.0 / math.sqrt(matrix_order)
    new_zeroth = None
    new_linear = None
    for iteration in range(STEPS):
        square, crossed = products(zeroth, linear)
        if iteration % 2 == 0:
            new_zeroth = kept_zero * (square * inv_root)
            new_linear = kept_first * (crossed * inv_root)
        else:
            new_zeroth = kept_zero * (2.0 * zeroth.astype(jnp.float32) - square * inv_root)
            new_linear = kept_first * (2.0 * linear.astype(jnp.float32) - crossed * inv_root)
        zeroth = new_zeroth.astype(jnp.bfloat16)
        linear = new_linear.astype(jnp.bfloat16)
    return (new_zeroth, new_linear)


def solution(mesh):
    return jax.shard_map(
        on_device,
        mesh=mesh,
        in_specs=(
            P("row", "col"),
            P(("row", "col"), None, None),
            P(("row", "col"), None),
            P(("row", "col")),
            P(("row", "col")),
            P(),
        ),
        out_specs=(P("row", "col"), P("row", "col")),
        check_vma=False,
    )
```

profile of v0, /device:TPU:0, one launch (start us, length us, event | category | flops | bytes accessed | tf_op | source)
XLA Modules:
  0.0 540.9 jit_solution(16579620292933018582)
XLA Ops:
  7.2 0.7 all-gather.11.cloned.1.call-update
  7.9 0.9 convert_reduce_fusion
  8.8 0.7 fusion.18
  9.5 1.1 scatter_custom_fusion.1
  10.6 0.8 all_to_all.17
  11.4 11.1 %all-to-all-start.1 = ((s32[128,1,2]{2,1,0:T(1,128)}), s32[128,1,2]{2,1,0:T(1,128)S(1)}, u32[]{:S(2)}, u32[]{:S(2)}) async-start(s32[128,1,2]{2,1,0:T(1,128)} %bitcast.10), calls=%async_computation.1 | async-start | bytes 131072 | tf_op jit(solution)/shard_map/all_to_all | solution.py:78
  22.5 0.8 fusion.23
  23.4 0.1 constant_dynamic-slice_fusion
  23.4 0.1 copy.44
  23.5 0.1 copy.45
  23.6 0.1 constant_dynamic-slice_fusion.2
  23.7 0.1 copy.41
  23.8 0.1 fusion.17
  23.9 1.1 scatter_custom_fusion
  25.0 0.8 all_to_all.15
  25.8 6.5 %all-to-all-done.1 = s32[128,1,2]{2,1,0:T(1,128)S(1)} async-done(((s32[128,1,2]{2,1,0:T(1,128)}), s32[128,1,2]{2,1,0:T(1,128)S(1)}, u32[]{:S(2)}, u32[]{:S(2)}) %all-to-all-start.1) | async-done | bytes 1056 | tf_op jit(solution)/shard_map/all_to_all | solution.py:78
  32.2 4.6 all-to-all-start
  36.8 0.1 broadcast_bitcast_fusion
  36.9 0.9 broadcast_in_dim.50
  37.8 13.4 %scatter_fusion = bf16[256,8,128]{2,1,0:T(8,128)(2,1)} fusion(bf16[256,8,128]{2,1,0:T(8,128)(2,1)} %broadcast_in_dim.50, s32[128]{0:T(128)S(1)} %fusion.18, bf16[128,8,128]{2,1,0:T(8,128)(2,1)S(1)} %copy-done.2), kind=kCustom, calls=%fused_computation.2 | custom fusion | bytes 786944 | tf_op jit(solution)/shard_map/scatter | solution.py:59
  51.1 0.5 broadcast.64
  51.7 0.8 reduce.6
  52.5 0.1 eq.91
  52.6 9.7 %all-to-all-start.2 = ((bf16[128,2,8,128]{3,2,1,0:T(8,128)(2,1)}), bf16[128,2,8,128]{3,2,1,0:T(8,128)(2,1)S(1)}, u32[]{:S(2)}, u32[]{:S(2)}) async-start(bf16[128,2,8,128]{3,2,1,0:T(8,128)(2,1)} %bitcast.13), calls=%async_computation.2 | async-start | bytes 1048576 | tf_op jit(solution)/shard_map/all_to_all | solution.py:64
  62.3 0.0 all-gather.19.cloned.1.call-start
  62.4 0.8 reduce.7
  63.2 0.1 eq.87
  63.3 0.1 broadcast_and_fusion
  63.5 0.1 and.26
  63.6 0.1 dot_general.34
  63.7 12.2 %all-to-all-done.2 = bf16[128,2,8,128]{3,2,1,0:T(8,128)(2,1)S(1)} async-done(((bf16[128,2,8,128]{3,2,1,0:T(8,128)(2,1)}), bf16[128,2,8,128]{3,2,1,0:T(8,128)(2,1)S(1)}, u32[]{:S(2)}, u32[]{:S(2)}) %all-to-all-start.2) | async-done | bytes 524320 | tf_op jit(solution)/shard_map/all_to_all | solution.py:64
  75.9 0.1 copy.71
  76.0 0.2 copy.48
  76.2 0.4 convolution_bitcast_fusion.1
  76.6 0.7 copy.70
  77.3 0.4 copy.51
  77.7 0.9 fusion.12
  78.6 0.0 all-gather.17.cloned.1.call-start
  78.7 0.7 all-gather.17.cloned.1.call-update
  79.4 0.5 all-gather.9.cloned.1.call-update
  79.9 0.0 all-gather.21.cloned.1.call-start
  80.0 0.1 broadcast_bitcast_fusion.1
  80.0 0.1 broadcast_in_dim.21
  80.1 0.4 copy.54
  80.5 69.7 %all-gather.19.cloned.1.call-done = bf16[768,6144]{0,1:T(8,128)(2,1)} async-done(((bf16[768,384]{0,1:T(8,128)(2,1)}), bf16[768,6144]{0,1:T(8,128)(2,1)}) %all-gather.19.cloned.1.call-update) | async-done | bytes 9437200 | tf_op jit(solution)/shard_map/all_gather | solution.py:27
  150.2 9.0 %fusion.24 = f32[768,384]{1,0:T(8,128)S(1)} fusion(bf16[768,6144]{0,1:T(8,128)(2,1)} %all-gather.19.cloned.1.call-done, bf16[6144,384]{1,0:T(8,128)(2,1)} %all-gather.11.cloned.1.call-done), kind=kOutput, calls=%fused_computation.56 | convolution fusion | flops 3623878656 | bytes 15335424 | tf_op jit(solution)/shard_map/dot_general | solution.py:31
  159.3 27.1 %all-gather.17.cloned.1.call-done = bf16[6144,384]{0,1:T(8,128)(2,1)} async-done(((bf16[768,384]{0,1:T(8,128)(2,1)}), bf16[6144,384]{0,1:T(8,128)(2,1)}) %all-gather.17.cloned.1.call-update) | async-done | bytes 4718608 | tf_op jit(solution)/shard_map/all_gather | solution.py:23
  186.4 85.9 %all-gather.9.cloned.1.call-done = bf16[768,6144]{1,0:T(8,128)(2,1)} async-done(((bf16[768,384]{1,0:T(8,128)(2,1)}), bf16[768,6144]{1,0:T(8,128)(2,1)}) %all-gather.9.cloned.1.call-update) | async-done | bytes 9437200 | tf_op jit(solution)/shard_map/all_gather | solution.py:26
  272.2 9.8 %fusion.9 = bf16[768,384]{1,0:T(8,128)(2,1)} fusion(f32[768,384]{1,0:T(8,128)S(1)} %copy.54, f32[768,384]{1,0:T(8,128)S(1)} %fusion.24, bf16[6144,384]{0,1:T(8,128)(2,1)} %all-gather.17.cloned.1.call-done, bf16[768,6144]{1,0:T(8,128)(2,1)} %all-gather.9.cloned.1.call-done), kind=kOutput, calls=%fused_computation.17 | convolution fusion | flops 3625058304 | bytes 17104896 | tf_op jit(solution)/shard_map/dot_general | solution.py:30
  282.1 0.2 all-gather.13.cloned.1.call-start
  282.3 0.1 broadcast_bitcast_fusion.2
  282.4 0.1 broadcast_in_dim.19
  282.5 0.4 copy.43
  282.8 9.7 %fusion.10 = bf16[768,384]{1,0:T(8,128)(2,1)} fusion(f32[768,384]{1,0:T(8,128)S(1)} %copy.43, bf16[768,6144]{1,0:T(8,128)(2,1)} %all-gather.9.cloned.1.call-done, bf16[6144,384]{1,0:T(8,128)(2,1)} %all-gather.11.cloned.1.call-done), kind=kOutput, calls=%fused_computation.18 | convolution fusion | flops 3624763392 | bytes 15925248 | tf_op jit(solution)/shard_map/dot_general | solution.py:29
  292.6 0.0 all-gather.15.cloned.1.call-start
  292.6 0.7 all-gather.15.cloned.1.call-update
  293.4 0.7 all-gather.23.cloned.1.call-update
  294.1 21.6 %all-gather.21.cloned.1.call-done = bf16[6144,384]{1,0:T(8,128)(2,1)} async-done(((bf16[768,384]{1,0:T(8,128)(2,1)}), bf16[6144,384]{1,0:T(8,128)(2,1)}) %all-gather.21.cloned.1.call-update) | async-done | bytes 4718608 | tf_op jit(solution)/shard_map/all_gather | solution.py:23
  315.7 86.4 %all-gather.13.cloned.1.call-done = bf16[768,6144]{1,0:T(8,128)(2,1)} async-done(((bf16[768,384]{1,0:T(8,128)(2,1)}), bf16[768,6144]{1,0:T(8,128)(2,1)}) %all-gather.13.cloned.1.call-update) | async-done | bytes 9437200 | tf_op jit(solution)/shard_map/all_gather | solution.py:26
  402.2 9.8 %fusion.25 = f32[768,384]{1,0:T(8,128)} fusion(bf16[768,6144]{1,0:T(8,128)(2,1)} %all-gather.13.cloned.1.call-done, bf16[6144,384]{1,0:T(8,128)(2,1)} %all-gather.21.cloned.1.call-done), kind=kOutput, calls=%fused_computation.57 | convolution fusion | flops 3623878656 | bytes 15335424 | tf_op jit(solution)/shard_map/dot_general | solution.py:30
  411.9 26.0 %all-gather.15.cloned.1.call-done = bf16[6144,384]{1,0:T(8,128)(2,1)} async-done(((bf16[768,384]{1,0:T(8,128)(2,1)}), bf16[6144,384]{1,0:T(8,128)(2,1)}) %all-gather.15.cloned.1.call-update) | async-done | bytes 4718608 | tf_op jit(solution)/shard_map/all_gather | solution.py:22
  438.0 9.8 %fusion.2 = f32[768,384]{1,0:T(8,128)} fusion(f32[768,384]{1,0:T(8,128)S(1)} %copy.43, bf16[768,6144]{1,0:T(8,128)(2,1)} %all-gather.13.cloned.1.call-done, bf16[6144,384]{1,0:T(8,128)(2,1)} %all-gather.15.cloned.1.call-done, bf16[768,384]{1,0:T(8,128)(2,1)S(1)} %copy-done.1), kind=kOutput, calls=%fused_computation.9 | convolution fusion | flops 3625353216 | bytes 17104896 | tf_op jit(solution)/shard_map/dot_general | solution.py:29
  447.8 76.2 %all-gather.23.cloned.1.call-done = bf16[768,6144]{1,0:T(8,128)(2,1)} async-done(((bf16[768,384]{1,0:T(8,128)(2,1)}), bf16[768,6144]{1,0:T(8,128)(2,1)}) %all-gather.23.cloned.1.call-update) | async-done | bytes 9437200 | tf_op jit(solution)/shard_map/all_gather | solution.py:27
  524.0 10.1 %fusion.8 = f32[768,384]{1,0:T(8,128)} fusion(f32[768,384]{1,0:T(8,128)S(1)} %copy.54, f32[768,384]{1,0:T(8,128)} %fusion.25, bf16[768,6144]{1,0:T(8,128)(2,1)} %all-gather.23.cloned.1.call-done, bf16[6144,384]{1,0:T(8,128)(2,1)} %all-gather.15.cloned.1.call-done, bf16[768,384]{1,0:T(8,128)(2,1)S(1)} %copy-done), kind=kOutput, calls=%fused_computation.16 | convolution fusion | flops 3625648128 | bytes 18284544 | tf_op jit(solution)/shard_map/dot_general | solution.py:31
  (21 shorter events, 0.3 us)
Async XLA Ops:
  7.2 30.6 %copy-start.2 = (bf16[128,8,128]{2,1,0:T(8,128)(2,1)S(1)}, bf16[128,8,128]{2,1,0:T(8,128)(2,1)}, u32[]{:S(2)}) copy-start(bf16[128,8,128]{2,1,0:T(8,128)(2,1)} %param.7) | copy-start | bytes 786436
  7.2 73.4 %all-gather.11.cloned.1.call-start = ((), (), s32[]{:S(2)}) async-start(), calls=%async_computation.4 | async-start | bytes 5308416 | tf_op jit(solution)/shard_map/all_gather | solution.py:22
  11.4 20.8 %all-to-all-start.1 = ((s32[128,1,2]{2,1,0:T(1,128)}), s32[128,1,2]{2,1,0:T(1,128)S(1)}, u32[]{:S(2)}, u32[]{:S(2)}) async-start(s32[128,1,2]{2,1,0:T(1,128)} %bitcast.10), calls=%async_computation.1 | async-start | bytes 131072 | tf_op jit(solution)/shard_map/all_to_all | solution.py:78
  32.2 20.4 %all-to-all-start = ((s32[128,1,2]{2,1,0:T(1,128)}), s32[128,1,2]{2,1,0:T(1,128)S(1)}, u32[]{:S(2)}, u32[]{:S(2)}) async-start(s32[128,1,2]{2,1,0:T(1,128)} %bitcast.9), calls=%async_computation | async-start | bytes 131072 | tf_op jit(solution)/shard_map/all_to_all | solution.py:71
  52.6 23.3 %all-to-all-start.2 = ((bf16[128,2,8,128]{3,2,1,0:T(8,128)(2,1)}), bf16[128,2,8,128]{3,2,1,0:T(8,128)(2,1)S(1)}, u32[]{:S(2)}, u32[]{:S(2)}) async-start(bf16[128,2,8,128]{3,2,1,0:T(8,128)(2,1)} %bitcast.13), calls=%async_computation.2 | async-start | bytes 1048576 | tf_op jit(solution)/shard_map/all_to_all | solution.py:64
  62.3 87.9 %all-gather.19.cloned.1.call-start = ((), (), s32[]{:S(2)}) async-start(), calls=%async_computation.8 | async-start | bytes 10027008 | tf_op jit(solution)/shard_map/all_gather | solution.py:27
  78.6 107.8 %all-gather.17.cloned.1.call-start = ((), (), s32[]{:S(2)}) async-start(), calls=%async_computation.7 | async-start | bytes 5308416 | tf_op jit(solution)/shard_map/all_gather | solution.py:23
  79.3 192.9 %all-gather.9.cloned.1.call-start = ((), (), s32[]{:S(2)}) async-start(), calls=%async_computation.3 | async-start | bytes 10027008 | tf_op jit(solution)/shard_map/all_gather | solution.py:26
  79.9 235.8 %all-gather.21.cloned.1.call-start = ((), (), s32[]{:S(2)}) async-start(), calls=%async_computation.9 | async-start | bytes 5308416 | tf_op jit(solution)/shard_map/all_gather | solution.py:23
  282.1 120.1 %all-gather.13.cloned.1.call-start = ((), (), s32[]{:S(2)}) async-start(), calls=%async_computation.5 | async-start | bytes 10027008 | tf_op jit(solution)/shard_map/all_gather | solution.py:26
  292.6 145.4 %all-gather.15.cloned.1.call-start = ((), (), s32[]{:S(2)}) async-start(), calls=%async_computation.6 | async-start | bytes 5308416 | tf_op jit(solution)/shard_map/all_gather | solution.py:22
  293.3 230.6 %all-gather.23.cloned.1.call-start = ((), (), s32[]{:S(2)}) async-start(), calls=%async_computation.10 | async-start | bytes 10027008 | tf_op jit(solution)/shard_map/all_gather | solution.py:27
  294.1 143.9 %copy-start.1 = (bf16[768,384]{1,0:T(8,128)(2,1)S(1)}, bf16[768,384]{1,0:T(8,128)(2,1)}, u32[]{:S(2)}) copy-start(bf16[768,384]{1,0:T(8,128)(2,1)} %fusion.10) | copy-start | bytes 1769476
  411.9 112.0 %copy-start = (bf16[768,384]{1,0:T(8,128)(2,1)S(1)}, bf16[768,384]{1,0:T(8,128)(2,1)}, u32[]{:S(2)}) copy-start(bf16[768,384]{1,0:T(8,128)(2,1)} %fusion.9) | copy-start | bytes 1769476
Sparse Core Ops, SparseCore 0:
  9.7 37.7 all-gather.10
  78.7 71.4 all-gather.18
  152.5 33.8 all-gather.16
  188.4 83.8 all-gather.8
  282.2 33.4 all-gather.20
  318.3 83.8 all-gather.12
  404.4 33.4 all-gather.14
  440.1 83.8 all-gather.22
where the time goes:
time: 541 us
  waiting for transfers between devices  415 us (77%)
  matrix products  58.5 us (11%)
  starting transfers between devices  25.9 us (5%)
  local copies, waits for them, and re-layouts  22.8 us (4%)
  between operations  14.4 us (3%)
    all_gather x2, waiting for transfers between devices, products(): lax.all_gather(zeroth, 'col', axis=1, tiled=True)  172 us
    all_gather x2, waiting for transfers between devices, products(): lax.all_gather(linear, 'col', axis=1, tiled=True)  146 us
    all_gather x2, waiting for transfers between devices, products(): lax.all_gather(linear, 'row', axis=0, tiled=True)  48.8 us
    all_gather x2, waiting for transfers between devices, products(): lax.all_gather(zeroth, 'row', axis=0, tiled=True)  26 us
    dot_general x2, matrix products, products(): jnp.dot(pieces[0], col_first, preferred_element_type=jnp.float32)  19.6 us
    dot_general x2, matrix products, products(): square = jnp.dot(pieces[0], col_zero, preferred_element_type=jnp.float32)  19.5 us
    dot_general x2, matrix products, products(): jnp.dot(pieces[1], col_zero, preferred_element_type=jnp.float32)  19.1 us
    scatter x1, local copies, waits for them, and re-layouts, on_device(): sent_strips = jnp.zeros((devices * capacity, atom_width, block_width), st...  13.4 us
  transfers between devices with their start and end apart: 11, of which 9 were waited for; matrix products, arithmetic and copies ran while one was open for 12% of the time, Pallas kernels for 0%

commit v1 on v0

--- a/solution.py
+++ b/solution.py
@@ -20,7 +20,9 @@
 def products(zeroth, linear):
     col_zero, col_first = (
         lax.all_gather(zeroth, "row", axis=0, tiled=True),
-        lax.all_gather(linear, "row", axis=0, tiled=True),
+        jnp.concatenate(
+            lax.all_to_all(jnp.stack([linear] * lax.axis_size("row")), "row", 0, 0), axis=0
+        ),
     )
     pieces = (
         lax.all_gather(zeroth, "col", axis=1, tiled=True),

time: 541 us -> 442 us (0.82)
  waiting for transfers between devices: 415 us -> 247 us
  blocking collectives: 0 us -> 60.2 us
    all_gather x2, waiting for transfers between devices: 172 us -> 65.4 us  [products(): lax.all_gather(zeroth, 'col', axis=1, tiled=True)]
    all_to_all x0 -> x1, blocking collectives: none -> 60.2 us  [products(): lax.all_to_all(jnp.stack([linear] * lax.axis_size('row')), 'row', 0, 0)]
    all_gather x2 -> x0, waiting for transfers between devices: 48.8 us -> none  [products(): lax.all_gather(linear, 'row', axis=0, tiled=True)]
    all_gather x2, waiting for transfers between devices: 146 us -> 135 us  [products(): lax.all_gather(linear, 'col', axis=1, tiled=True)]
  transfers between devices with their start and end apart: 11 -> 10, of which waited for: 9 -> 7; matrix products, arithmetic and copies ran while one was open for 12% -> 17% of each run, Pallas kernels for 0% -> 0%
where the time goes in v1:
time: 442 us; the launch traced here: 441 us
  waiting for transfers between devices  247 us (56%)
  blocking collectives  60.2 us (14%)
  matrix products  59.2 us (13%)
  starting transfers between devices  30.5 us (7%)
  local copies, waits for them, and re-layouts  26.8 us (6%)
  between operations  14.4 us (3%)
    all_gather x2, waiting for transfers between devices, products(): lax.all_gather(linear, 'col', axis=1, tiled=True)  135 us
    all_gather x2, waiting for transfers between devices, products(): lax.all_gather(zeroth, 'col', axis=1, tiled=True)  65.4 us
    all_to_all x1, blocking collectives, products(): lax.all_to_all(jnp.stack([linear] * lax.axis_size('row')), 'row', 0, 0)  60.2 us
    all_gather x2, waiting for transfers between devices, products(): lax.all_gather(zeroth, 'row', axis=0, tiled=True)  25.8 us
    dot_general x2, matrix products, products(): jnp.dot(pieces[0], col_first, preferred_element_type=jnp.float32)  20 us
    dot_general x2, matrix products, products(): square = jnp.dot(pieces[0], col_zero, preferred_element_type=jnp.float32)  19.5 us
    dot_general x2, matrix products, products(): jnp.dot(pieces[1], col_zero, preferred_element_type=jnp.float32)  19.3 us
    scatter x1, local copies, waits for them, and re-layouts, on_device(): sent_strips = jnp.zeros((devices * capacity, atom_width, block_width), st...  13.3 us
  transfers between devices with their start and end apart: 10, of which 7 were waited for; matrix products, arithmetic and copies ran while one was open for 17% of the time, Pallas kernels for 0%

profile of v1, /device:TPU:0, one launch (start us, length us, event | category | flops | bytes accessed | tf_op | source)
XLA Modules:
  0.0 440.9 jit_solution(8285399760148214577)
XLA Ops:
  7.2 0.7 all-gather.9.cloned.1.call-update
  7.9 0.0 all-gather.7.cloned.1.call-start
  8.0 0.7 all-gather.7.cloned.1.call-update
  8.7 0.2 convert_reduce_fusion
  8.9 1.1 scatter_custom_fusion.1
  10.0 0.8 all_to_all.23
  10.8 11.1 %all-to-all-start.1 = ((s32[128,1,2]{2,1,0:T(1,128)}), s32[128,1,2]{2,1,0:T(1,128)S(1)}, u32[]{:S(2)}, u32[]{:S(2)}) async-start(s32[128,1,2]{2,1,0:T(1,128)} %bitcast.10), calls=%async_computation.1 | async-start | bytes 131072 | tf_op jit(solution)/shard_map/all_to_all | solution.py:80
  21.9 0.1 constant_dynamic-slice_fusion
  22.0 0.1 copy.46
  22.1 0.1 copy.47
  22.2 0.1 constant_dynamic-slice_fusion.2
  22.3 0.1 copy.43
  22.4 0.1 fusion.17
  22.5 1.1 scatter_custom_fusion
  23.6 0.8 all_to_all.21
  24.4 7.0 %all-to-all-done.1 = s32[128,1,2]{2,1,0:T(1,128)S(1)} async-done(((s32[128,1,2]{2,1,0:T(1,128)}), s32[128,1,2]{2,1,0:T(1,128)S(1)}, u32[]{:S(2)}, u32[]{:S(2)}) %all-to-all-start.1) | async-done | bytes 1056 | tf_op jit(solution)/shard_map/all_to_all | solution.py:80
  31.3 4.6 %all-to-all-start = ((s32[128,1,2]{2,1,0:T(1,128)}), s32[128,1,2]{2,1,0:T(1,128)S(1)}, u32[]{:S(2)}, u32[]{:S(2)}) async-start(s32[128,1,2]{2,1,0:T(1,128)} %bitcast.9), calls=%async_computation | async-start | bytes 131072 | tf_op jit(solution)/shard_map/all_to_all | solution.py:73
  35.9 0.1 broadcast_bitcast_fusion
  36.0 0.9 broadcast_in_dim.50
  36.9 13.3 %scatter_fusion = bf16[256,8,128]{2,1,0:T(8,128)(2,1)} fusion(bf16[256,8,128]{2,1,0:T(8,128)(2,1)} %broadcast_in_dim.50, s32[128]{0:T(128)S(1)} %fusion.18, bf16[128,8,128]{2,1,0:T(8,128)(2,1)S(1)} %copy-done.3), kind=kCustom, calls=%fused_computation.2 | custom fusion | bytes 786944 | tf_op jit(solution)/shard_map/scatter | solution.py:61
  50.2 0.5 broadcast.67
  50.7 0.7 reduce.6
  51.4 0.1 eq.91
  51.6 9.8 %all-to-all-start.2 = ((bf16[128,2,8,128]{3,2,1,0:T(8,128)(2,1)}), bf16[128,2,8,128]{3,2,1,0:T(8,128)(2,1)S(1)}, u32[]{:S(2)}, u32[]{:S(2)}) async-start(bf16[128,2,8,128]{3,2,1,0:T(8,128)(2,1)} %bitcast.13), calls=%async_computation.2 | async-start | bytes 1048576 | tf_op jit(solution)/shard_map/all_to_all | solution.py:66
  61.4 0.0 all-gather.15.cloned.1.call-start
  61.4 0.7 reduce.7
  62.1 0.1 eq.87
  62.3 0.1 broadcast_and_fusion
  62.4 0.1 and.26
  62.6 0.1 dot_general.34
  62.7 12.3 %all-to-all-done.2 = bf16[128,2,8,128]{3,2,1,0:T(8,128)(2,1)S(1)} async-done(((bf16[128,2,8,128]{3,2,1,0:T(8,128)(2,1)}), bf16[128,2,8,128]{3,2,1,0:T(8,128)(2,1)S(1)}, u32[]{:S(2)}, u32[]{:S(2)}) %all-to-all-start.2) | async-done | bytes 524320 | tf_op jit(solution)/shard_map/all_to_all | solution.py:66
  75.0 0.1 copy.74
  75.1 0.2 copy.50
  75.3 0.4 convolution_bitcast_fusion.1
  75.6 0.7 copy.73
  76.3 0.4 copy.53
  76.7 0.9 fusion.12
  77.7 0.0 all-gather.11.cloned.1.call-start
  77.7 0.1 broadcast_bitcast_fusion.2
  77.8 0.1 broadcast_in_dim.19
  77.9 0.4 copy.45
  78.3 60.5 %all-gather.7.cloned.1.call-done = bf16[768,6144]{1,0:T(8,128)(2,1)} async-done(((bf16[768,384]{1,0:T(8,128)(2,1)}), bf16[768,6144]{1,0:T(8,128)(2,1)}) %all-gather.7.cloned.1.call-update) | async-done | bytes 9437200 | tf_op jit(solution)/shard_map/all_gather | solution.py:28
  138.8 9.7 %fusion.10 = bf16[768,384]{1,0:T(8,128)(2,1)} fusion(f32[768,384]{1,0:T(8,128)S(1)} %copy.45, bf16[768,6144]{1,0:T(8,128)(2,1)} %all-gather.7.cloned.1.call-done, bf16[6144,384]{1,0:T(8,128)(2,1)} %all-gather.9.cloned.1.call-done), kind=kOutput, calls=%fused_computation.18 | convolution fusion | flops 3624763392 | bytes 15925248 | tf_op jit(solution)/shard_map/dot_general | solution.py:31
  148.5 0.0 all-gather.13.cloned.1.call-start
  148.6 0.5 all-gather.13.cloned.1.call-update
  149.1 0.4 copy-done
  149.6 0.3 copy.54
  149.9 2.6 stack.4
  152.5 4.6 %all-to-all-start.3 = ((bf16[8,768,384]{2,1,0:T(8,128)(2,1)}), bf16[8,768,384]{2,1,0:T(8,128)(2,1)}, u32[]{:S(2)}, u32[]{:S(2)}) async-start(bf16[8,768,384]{2,1,0:T(8,128)(2,1)} %stack.4), calls=%async_computation.3 | async-start | bytes 9437184 | tf_op jit(solution)/shard_map/all_to_all | solution.py:24
  157.1 0.2 all-gather.17.cloned.1.call-start
  157.3 0.1 broadcast_bitcast_fusion.1
  157.4 0.1 broadcast_in_dim.21
  157.5 0.4 copy.57
  157.9 58.6 %all-gather.15.cloned.1.call-done = bf16[768,6144]{0,1:T(8,128)(2,1)} async-done(((bf16[768,384]{0,1:T(8,128)(2,1)}), bf16[768,6144]{0,1:T(8,128)(2,1)}) %all-gather.15.cloned.1.call-update) | async-done | bytes 9437200 | tf_op jit(solution)/shard_map/all_gather | solution.py:29
  216.5 9.2 %fusion.24 = f32[768,384]{1,0:T(8,128)S(1)} fusion(bf16[768,6144]{0,1:T(8,128)(2,1)} %all-gather.15.cloned.1.call-done, bf16[6144,384]{1,0:T(8,128)(2,1)} %all-gather.9.cloned.1.call-done), kind=kOutput, calls=%fused_computation.56 | convolution fusion | flops 3623878656 | bytes 15335424 | tf_op jit(solution)/shard_map/dot_general | solution.py:33
  225.7 10.2 %fusion.9 = bf16[768,384]{1,0:T(8,128)(2,1)} fusion(f32[768,384]{1,0:T(8,128)S(1)} %copy.57, f32[768,384]{1,0:T(8,128)S(1)} %fusion.24, bf16[768,6144]{1,0:T(8,128)(2,1)} %all-gather.7.cloned.1.call-done, bf16[6144,384]{1,0:T(8,128)(2,1)} %bitcast.19), kind=kOutput, calls=%fused_computation.17 | convolution fusion | flops 3625058304 | bytes 17104896 | tf_op jit(solution)/shard_map/dot_general | solution.py:32
  235.9 1.5 stack.5
  237.4 60.2 %all_to_all.33 = bf16[8,768,384]{2,1,0:T(8,128)(2,1)} all-to-all(bf16[8,768,384]{2,1,0:T(8,128)(2,1)S(1)} %stack.5), channel_id=1, replica_groups=mesh['row'=8,'col'=16] {'row'}, dimensions={0} | all-to-all | bytes 9437184 | tf_op jit(solution)/shard_map/all_to_all | solution.py:24
  297.6 4.9 %all-gather.11.cloned.1.call-done = bf16[768,6144]{1,0:T(8,128)(2,1)} async-done(((bf16[768,384]{1,0:T(8,128)(2,1)}), bf16[768,6144]{1,0:T(8,128)(2,1)}) %all-gather.11.cloned.1.call-update) | async-done | bytes 9437200 | tf_op jit(solution)/shard_map/all_gather | solution.py:28
  302.5 9.8 %fusion.25 = f32[768,384]{1,0:T(8,128)} fusion(bf16[768,6144]{1,0:T(8,128)(2,1)} %all-gather.11.cloned.1.call-done, bf16[6144,384]{1,0:T(8,128)(2,1)} %bitcast.90), kind=kOutput, calls=%fused_computation.57 | convolution fusion | flops 3623878656 | bytes 15335424 | tf_op jit(solution)/shard_map/dot_general | solution.py:32
  312.3 25.8 %all-gather.13.cloned.1.call-done = bf16[6144,384]{1,0:T(8,128)(2,1)} async-done(((bf16[768,384]{1,0:T(8,128)(2,1)}), bf16[6144,384]{1,0:T(8,128)(2,1)}) %all-gather.13.cloned.1.call-update) | async-done | bytes 4718608 | tf_op jit(solution)/shard_map/all_gather | solution.py:22
  338.1 9.8 %fusion.2 = f32[768,384]{1,0:T(8,128)} fusion(f32[768,384]{1,0:T(8,128)S(1)} %copy.45, bf16[768,6144]{1,0:T(8,128)(2,1)} %all-gather.11.cloned.1.call-done, bf16[6144,384]{1,0:T(8,128)(2,1)} %all-gather.13.cloned.1.call-done, bf16[768,384]{1,0:T(8,128)(2,1)S(1)} %copy-done.1), kind=kOutput, calls=%fused_computation.9 | convolution fusion | flops 3625353216 | bytes 17104896 | tf_op jit(solution)/shard_map/dot_general | solution.py:31
  347.9 76.1 %all-gather.17.cloned.1.call-done = bf16[768,6144]{1,0:T(8,128)(2,1)} async-done(((bf16[768,384]{1,0:T(8,128)(2,1)}), bf16[768,6144]{1,0:T(8,128)(2,1)}) %all-gather.17.cloned.1.call-update) | async-done | bytes 9437200 | tf_op jit(solution)/shard_map/all_gather | solution.py:29
  424.0 10.1 %fusion.8 = f32[768,384]{1,0:T(8,128)} fusion(f32[768,384]{1,0:T(8,128)S(1)} %copy.57, f32[768,384]{1,0:T(8,128)} %fusion.25, bf16[768,6144]{1,0:T(8,128)(2,1)} %all-gather.17.cloned.1.call-done, bf16[6144,384]{1,0:T(8,128)(2,1)} %all-gather.13.cloned.1.call-done, bf16[768,384]{1,0:T(8,128)(2,1)S(1)} %copy-done.2), kind=kOutput, calls=%fused_computation.16 | convolution fusion | flops 3625648128 | bytes 18284544 | tf_op jit(solution)/shard_map/dot_general | solution.py:33
  (27 shorter events, 0.2 us)
Async XLA Ops:
  7.2 1.5 copy-start.5
  7.2 14.7 %copy-start.4 = (s32[3,48,48]{2,1,0:T(8,128)S(1)}, s32[3,48,48]{2,1,0:T(8,128)}, u32[]{:S(2)}) copy-start(s32[3,48,48]{2,1,0:T(8,128)} %param.11) | copy-start | bytes 82948
  7.2 29.7 %copy-start.3 = (bf16[128,8,128]{2,1,0:T(8,128)(2,1)S(1)}, bf16[128,8,128]{2,1,0:T(8,128)(2,1)}, u32[]{:S(2)}) copy-start(bf16[128,8,128]{2,1,0:T(8,128)(2,1)} %param.7) | copy-start | bytes 786436
  7.2 71.1 %all-gather.9.cloned.1.call-start = ((), (), s32[]{:S(2)}) async-start(), calls=%async_computation.6 | async-start | bytes 5308416 | tf_op jit(solution)/shard_map/all_gather | solution.py:22
  7.9 130.9 %all-gather.7.cloned.1.call-start = ((), (), s32[]{:S(2)}) async-start(), calls=%async_computation.5 | async-start | bytes 10027008 | tf_op jit(solution)/shard_map/all_gather | solution.py:28
  10.8 20.6 %all-to-all-start.1 = ((s32[128,1,2]{2,1,0:T(1,128)}), s32[128,1,2]{2,1,0:T(1,128)S(1)}, u32[]{:S(2)}, u32[]{:S(2)}) async-start(s32[128,1,2]{2,1,0:T(1,128)} %bitcast.10), calls=%async_computation.1 | async-start | bytes 131072 | tf_op jit(solution)/shard_map/all_to_all | solution.py:80
  31.3 20.3 %all-to-all-start = ((s32[128,1,2]{2,1,0:T(1,128)}), s32[128,1,2]{2,1,0:T(1,128)S(1)}, u32[]{:S(2)}, u32[]{:S(2)}) async-start(s32[128,1,2]{2,1,0:T(1,128)} %bitcast.9), calls=%async_computation | async-start | bytes 131072 | tf_op jit(solution)/shard_map/all_to_all | solution.py:73
  51.6 23.4 %all-to-all-start.2 = ((bf16[128,2,8,128]{3,2,1,0:T(8,128)(2,1)}), bf16[128,2,8,128]{3,2,1,0:T(8,128)(2,1)S(1)}, u32[]{:S(2)}, u32[]{:S(2)}) async-start(bf16[128,2,8,128]{3,2,1,0:T(8,128)(2,1)} %bitcast.13), calls=%async_computation.2 | async-start | bytes 1048576 | tf_op jit(solution)/shard_map/all_to_all | solution.py:66
  61.4 155.1 %all-gather.15.cloned.1.call-start = ((), (), s32[]{:S(2)}) async-start(), calls=%async_computation.9 | async-start | bytes 10027008 | tf_op jit(solution)/shard_map/all_gather | solution.py:29
  77.7 224.8 %all-gather.11.cloned.1.call-start = ((), (), s32[]{:S(2)}) async-start(), calls=%async_computation.7 | async-start | bytes 10027008 | tf_op jit(solution)/shard_map/all_gather | solution.py:28
  148.5 1.1 copy-start
  148.5 189.6 %all-gather.13.cloned.1.call-start = ((), (), s32[]{:S(2)}) async-start(), calls=%async_computation.8 | async-start | bytes 5308416 | tf_op jit(solution)/shard_map/all_gather | solution.py:22
  152.5 73.2 %all-to-all-start.3 = ((bf16[8,768,384]{2,1,0:T(8,128)(2,1)}), bf16[8,768,384]{2,1,0:T(8,128)(2,1)}, u32[]{:S(2)}, u32[]{:S(2)}) async-start(bf16[8,768,384]{2,1,0:T(8,128)(2,1)} %stack.4), calls=%async_computation.3 | async-start | bytes 9437184 | tf_op jit(solution)/shard_map/all_to_all | solution.py:24
  157.1 266.9 %all-gather.17.cloned.1.call-start = ((), (), s32[]{:S(2)}) async-start(), calls=%async_computation.10 | async-start | bytes 10027008 | tf_op jit(solution)/shard_map/all_gather | solution.py:29
  302.5 35.6 %copy-start.1 = (bf16[768,384]{1,0:T(8,128)(2,1)S(1)}, bf16[768,384]{1,0:T(8,128)(2,1)}, u32[]{:S(2)}) copy-start(bf16[768,384]{1,0:T(8,128)(2,1)} %fusion.10) | copy-start | bytes 1769476
  312.3 111.7 %copy-start.2 = (bf16[768,384]{1,0:T(8,128)(2,1)S(1)}, bf16[768,384]{1,0:T(8,128)(2,1)}, u32[]{:S(2)}) copy-start(bf16[768,384]{1,0:T(8,128)(2,1)} %fusion.9) | copy-start | bytes 1769476
Sparse Core Ops, SparseCore 0:
  9.7 37.4 all-gather.8
  49.3 89.4 all-gather.6
  141.5 74.9 all-gather.14
  219.0 83.4 all-gather.10
  304.6 33.4 all-gather.12
  340.1 83.8 all-gather.16
